TPU v7x, 32 devices: a whole 2x2x4 slice. The times are simulated.
32 devices in a mesh: grp: 2 (over x), elem: 8 (over z, y), lev: 2 (over core).
Axes of the slice: x: 2, y: 2, z: 4, core: 2. Of those that a mesh axis runs over, the one named last changes fastest.
Arguments:
- tracer_field: float32 [2, 48, 16, 4096], P(None, 'lev', None, ('grp', 'elem')), parts along dimension 3, may hold values from -6 to 6
- velocity: float32 [2, 48, 16, 4096], P(None, 'lev', None, ('grp', 'elem')), parts along dimension 3, may hold values from -3 to 3
- node_mass: float32 [16, 4096], P(None, ('grp', 'elem')), parts along dimension 1, may hold values from 0.5 to 2
- neighbours: int32 [4, 4096], P(None, ('grp', 'elem')), parts along dimension 1, may hold values from 0 to 2047, as said below
- seam_flips: int32 [4, 4096], P(None, ('grp', 'elem')), parts along dimension 1, may hold values from 0 to 1, as said below
- conv_in: float32 [3, 16, 4], replicated, may hold values from -1.75 to 1.75
- bias_in: float32 [16], replicated, may hold values from -3 to 3
- conv_out: float32 [3, 2, 16], replicated, may hold values from -0.875 to 0.875
- bias_out: float32 [2], replicated, may hold values from -3 to 3
Outputs:
- tracer_next: float32 [2, 48, 16, 4096], P(None, 'lev', None, ('grp', 'elem')), parts along dimension 3
- subgrid: float32 [2, 48, 4, 4096], P(None, 'lev', None, ('grp', 'elem')), parts along dimension 3
There are 2 independent parts, one for each index of `grp`. A program takes and returns all parts, laid end to end along the dimension named above; an argument that names none is the same for every part. Nothing has to cross between parts.
Inputs may be any that keep to these rules, and one draw needn't show every extreme that they name: Across edge k, element e touches edge (k + 2) mod 4 of element neighbours[k, e], and neighbours[(k + 2) mod 4, neighbours[k, e]] is e. Elements are numbered so that index j of elem owns elements j * 256 to (j + 1) * 256 - 1; the neighbours across edges 1 and 3 are owned by the same index of elem, those across edges 0 and 2 by the same index or the next or previous one, cyclically; across edge 0 never the next one and across edge 2 never the previous one. seam_flips[k, e] equals seam_flips[(k + 2) mod 4, neighbours[k, e]].
All inputs are finite; a program needn't handle non-finite values.
Results may differ from a plain program's by a relative error of at most 0.0001.
Values sent between devices are 32-bit elements; how exact they have to be, the bound alone decides.
A program may use at most 64 MiB of HBM per device.

v0:
```python
import functools

import jax
import jax.numpy as jnp
import numpy as np
from jax import lax
from jax.experimental import pallas as pl
from jax.experimental.pallas import tpu as pltpu
from jax.sharding import PartitionSpec as P

TIME_STEP = 0.1
EDGE_NODES = ((0, 1, 2, 3), (3, 7, 11, 15), (12, 13, 14, 15), (0, 4, 8, 12))
MESH = pl.DeviceIdType.MESH
SUB = 8
GUARD = 16


def derivative_matrix():
    points = np.array([-1.0, -1.0 / np.sqrt(5.0), 1.0 / np.sqrt(5.0), 1.0])
    bary = [
        1.0 / np.prod([points[i] - points[k] for k in range(4) if k != i]) for i in range(4)
    ]
    matrix = np.zeros((4, 4))
    for i in range(4):
        for j in range(4):
            if i != j:
                matrix[i, j] = bary[j] / bary[i] / (points[i] - points[j])
        matrix[i, i] = -np.sum(matrix[i])
    matrix[np.abs(matrix) < 1e-12] = 0.0
    return matrix


def gathered(values, table, parts):
    rows = values.shape[0]
    pieces, rest = [], values
    for _ in range(parts):
        piece = rest.astype(jnp.bfloat16)
        pieces.append(piece)
        rest = rest - piece.astype(jnp.float32)
    out = jnp.dot(jnp.concatenate(pieces, axis=0), table, preferred_element_type=jnp.float32)
    total = out[:rows]
    for part in range(1, parts):
        total = total + out[part * rows : (part + 1) * rows]
    return total


def kernel(
    devices, tracer_in, velocity_in, mass, nbr, flips, conv_in, bias_in, conv_out, bias_out,
    next_out, sub_out,
    start, now, wind, weighted, base, landed, inv, cell_inv, tables, mass_land, features, partial,
    in_sem, send_sem, recv_sem, mass_send_sem, mass_recv_sem, col_send_sem, col_recv_sem,
):
    local = mass.shape[1]
    levels = start.shape[2]
    chunks = levels // SUB
    matrix = derivative_matrix()
    me, lev = lax.axis_index("elem"), lax.axis_index("lev")
    after, before = lax.rem(me + 1, devices), lax.rem(me + devices - 1, devices)

    loads = []
    for node in range(16):
        loads.append(
            pltpu.make_async_copy(tracer_in.at[:, :, node, :], start.at[node], in_sem.at[0, node])
        )
        loads.append(
            pltpu.make_async_copy(velocity_in.at[:, :, node, :], wind.at[node], in_sem.at[1, node])
        )
    for load in loads:
        load.start()

    barrier = pltpu.get_barrier_semaphore()
    for device in ({"elem": before}, {"elem": after}, {"lev": 1 - lev}):
        pl.semaphore_signal(barrier, inc=1, device_id=device, device_id_type=MESH)

    rows = lax.broadcasted_iota(jnp.int32, (local, local), 0)
    for slot, (edge, owner) in enumerate(
        ((0, me), (1, me), (2, me), (3, me), (0, before), (2, after))
    ):
        wanted = nbr[pl.ds(edge, 1), :] - owner * local
        tables[slot] = jnp.where(rows == wanted, 1.0, 0.0).astype(jnp.bfloat16)
    pl.semaphore_wait(barrier, 3)

    mass_copies = []
    for side, device in ((0, after), (1, before)):
        mass_copies.append(
            pltpu.make_async_remote_copy(
                src_ref=mass.at[pl.ds(8 * (1 - side), 8), :],
                dst_ref=mass_land.at[side],
                send_sem=mass_send_sem.at[side],
                recv_sem=mass_recv_sem.at[side],
                device_id={"elem": device},
                device_id_type=MESH,
            )
        )
        mass_copies[-1].start()

    def edge_copy(side, step):
        return pltpu.make_async_remote_copy(
            src_ref=weighted.at[step, pl.ds(12 if side == 0 else 0, 4)],
            dst_ref=landed.at[side, step],
            send_sem=send_sem.at[side, step],
            recv_sem=recv_sem.at[side, step],
            device_id={"elem": after if side == 0 else before},
            device_id_type=MESH,
        )

    def place(chunk):
        return pl.multiple_of(jnp.where(lev == 0, chunks - 1 - chunk, chunk) * SUB, SUB)

    def is_flipped(edge):
        return flips[pl.ds(edge, 1), :] == 1

    def slopes(field, chunk, step):
        at = pl.ds(place(chunk), SUB)
        for tracer in range(2):
            q = [field[node, tracer, at, :] for node in range(16)]
            for node in (12, 13, 14, 15, 0, 1, 2, 3, 4, 5, 6, 7, 8, 9, 10, 11):
                iy, ix = divmod(node, 4)
                along_x = sum(float(matrix[ix, j]) * q[4 * iy + j] for j in range(4) if matrix[ix, j])
                along_y = sum(float(matrix[iy, j]) * q[4 * j + ix] for j in range(4) if matrix[iy, j])
                weighted[step, node, tracer] = (
                    wind[node, 0, at, :] * along_x + wind[node, 1, at, :] * along_y
                )
        edge_copy(0, step).start()
        edge_copy(1, step).start()
        arrivals = [[] for _ in range(16)]
        for edge in range(4):
            theirs = EDGE_NODES[(edge + 2) % 4]
            source = jnp.concatenate(
                [weighted[step, node].reshape(2 * SUB, local) for node in theirs], axis=0
            )
            settle(arrivals, edge, gathered(source, tables[edge], 2))
        for node in range(16):
            total = weighted[step, node].reshape(2 * SUB, local)
            for arrived in arrivals[node]:
                total = total + arrived
            base[chunk, node] = total.reshape(2, SUB, local)

    def settle(arrivals, edge, arrived):
        count = arrived.shape[0] // 4
        flip = is_flipped(edge)
        for slot, node in enumerate(EDGE_NODES[edge]):
            arrivals[node].append(
                jnp.where(
                    flip,
                    arrived[(3 - slot) * count : (4 - slot) * count],
                    arrived[slot * count : (slot + 1) * count],
                )
            )

    def finish(chunk, step, keep, blend):
        at = pl.ds(place(chunk), SUB)
        edge_copy(0, step).wait_recv()
        edge_copy(1, step).wait_recv()
        arrivals = [[] for _ in range(16)]
        for side, edge in ((0, 0), (1, 2)):
            source = landed[side, step].reshape(8 * SUB, local)
            settle(arrivals, edge, gathered(source, tables[4 + side], 2))
        for node in range(16):
            total = base[chunk, node].reshape(2 * SUB, local)
            for arrived in arrivals[node]:
                total = total + arrived
            total = total.reshape(2, SUB, local)
            for tracer in range(2):
                section = now[node, tracer, at, :] + TIME_STEP * inv[node] * total[tracer]
                now[node, tracer, at, :] = keep * start[node, tracer, at, :] + blend * section

    for load in loads:
        load.wait()

    def prepare(chunk, carry):
        at = pl.ds(place(chunk), SUB)
        for node in range(16):
            node_mass = mass[pl.ds(node, 1), :]
            for way in range(2):
                wind[node, way, at, :] = -(wind[node, way, at, :] * node_mass)
            for tracer in range(2):
                now[node, tracer, at, :] = start[node, tracer, at, :]
        slopes(start, chunk, chunk)
        return carry

    lax.fori_loop(0, chunks, prepare, 0)

    own_mass = mass[...]
    sums = [own_mass[node : node + 1] for node in range(16)]
    own = [
        gathered(own_mass[8:16], tables[0], 3),
        gathered(own_mass, tables[1], 3),
        gathered(own_mass[0:8], tables[2], 3),
        gathered(own_mass, tables[3], 3),
    ]
    for side in range(2):
        mass_copies[side].wait_recv()
    far = [gathered(mass_land[side], tables[4 + side], 3) for side in range(2)]
    own[0] = own[0] + far[0]
    own[2] = own[2] + far[1]
    for edge in range(4):
        theirs = EDGE_NODES[(edge + 2) % 4]
        shift = 8 if edge == 0 else 0
        flip = is_flipped(edge)
        for slot, node in enumerate(EDGE_NODES[edge]):
            straight, turned = theirs[slot] - shift, theirs[3 - slot] - shift
            sums[node] = sums[node] + jnp.where(
                flip, own[edge][turned : turned + 1], own[edge][straight : straight + 1]
            )
    for node in range(16):
        inv[node] = jnp.broadcast_to(1.0 / sums[node], (SUB, local))
    cells = [
        [4 * (2 * (cell // 2) + dy) + 2 * (cell % 2) + dx for dy in range(2) for dx in range(2)]
        for cell in range(4)
    ]
    for cell in range(4):
        cell_mass = sum(own_mass[node : node + 1] for node in cells[cell])
        cell_inv[cell] = jnp.broadcast_to(1.0 / cell_mass, (SUB, local))

    nothing = jnp.zeros((SUB, local), jnp.float32)
    open_side = pl.multiple_of(jnp.where(lev == 0, GUARD - SUB, GUARD + levels), SUB)
    for cell in range(4):
        for channel in range(4):
            features[channel, cell, pl.ds(0, SUB), :] = nothing
            features[channel, cell, pl.ds(GUARD + levels + SUB, SUB), :] = nothing
            features[channel, cell, pl.ds(open_side, SUB), :] = nothing
        for kind in range(6):
            partial[kind, cell, pl.ds(open_side, SUB), :] = nothing

    def section_step(index, carry):
        chunk = lax.rem(index, chunks)
        first, second = index < chunks, index < 2 * chunks
        keep = jnp.where(first, 0.0, jnp.where(second, 0.75, 1.0 / 3.0)).astype(jnp.float32)
        blend = jnp.where(first, 1.0, jnp.where(second, 0.25, 2.0 / 3.0)).astype(jnp.float32)
        finish(chunk, index, keep, blend)

        @pl.when(second)
        def _():
            slopes(now, chunk, index + chunks)

        return carry

    lax.fori_loop(0, 2 * chunks, section_step, 0)

    column_copy = pltpu.make_async_remote_copy(
        src_ref=features.at[:, :, pl.ds(pl.multiple_of(GUARD + place(0), SUB), SUB), :],
        dst_ref=features.at[
            :, :, pl.ds(pl.multiple_of(jnp.where(lev == 0, GUARD - SUB, GUARD + levels), SUB), SUB), :
        ],
        send_sem=col_send_sem,
        recv_sem=col_recv_sem,
        device_id={"lev": 1 - lev},
        device_id_type=MESH,
    )

    def last_step(index, carry):
        chunk = index - 2 * chunks
        finish(chunk, index, jnp.float32(1.0 / 3.0), jnp.float32(2.0 / 3.0))
        at = pl.ds(place(chunk), SUB)
        column = pl.ds(pl.multiple_of(GUARD + place(chunk), SUB), SUB)
        for cell in range(4):
            for tracer in range(2):
                features[tracer, cell, column, :] = cell_inv[cell] * sum(
                    mass[pl.ds(node, 1), :] * now[node, tracer, at, :] for node in cells[cell]
                )
                features[2 + tracer, cell, column, :] = -cell_inv[cell] * sum(
                    wind[node, tracer, at, :] for node in cells[cell]
                )
        for node in range(16):
            for tracer in range(2):
                next_out[node, tracer, at, :] = now[node, tracer, at, :]

        @pl.when(chunk == 0)
        def _():
            column_copy.start()

        return carry

    lax.fori_loop(2 * chunks, 3 * chunks, last_step, 0)
    column_copy.wait()

    def column_net(index, carry):
        chunk, cell = index // 4, lax.rem(index, 4)
        inner = GUARD + chunk * SUB
        border = jnp.where(lev == 0, GUARD + levels, GUARD - SUB)
        at = pl.multiple_of(jnp.where(chunk < chunks, inner, border), SUB)
        inputs = []
        for channel in range(4):
            whole = features[channel, cell, pl.ds(pl.multiple_of(at - SUB, SUB), 3 * SUB), :]
            inputs.append([whole[SUB - 1 + j : 2 * SUB - 1 + j] for j in range(3)])
        totals = [None] * 6
        for out in range(16):
            value = bias_in[out]
            for j in range(3):
                for channel in range(4):
                    value = value + conv_in[j, out, channel] * inputs[channel][j]
            value = value / (1.0 + jnp.exp(-value))
            for j in range(3):
                for tracer in range(2):
                    term = conv_out[j, tracer, out] * value
                    kind = 2 * j + tracer
                    totals[kind] = term if totals[kind] is None else totals[kind] + term
        for kind in range(6):
            partial[kind, cell, pl.ds(at, SUB), :] = totals[kind]
        return carry

    lax.fori_loop(0, 4 * (chunks + 1), column_net, 0)

    for cell in range(4):
        for tracer in range(2):
            sub_out[tracer, cell] = (
                bias_out[tracer]
                + partial[tracer, cell, pl.ds(GUARD - 1, levels), :]
                + partial[2 + tracer, cell, pl.ds(GUARD, levels), :]
                + partial[4 + tracer, cell, pl.ds(GUARD + 1, levels), :]
            )

    def drain(index, carry):
        edge_copy(0, index).wait_send()
        edge_copy(1, index).wait_send()
        return carry

    lax.fori_loop(0, 3 * chunks, drain, 0)
    for side in range(2):
        mass_copies[side].wait_send()


def per_device(
    tracer_field, velocity, node_mass, neighbours, seam_flips, conv_in, bias_in, conv_out, bias_out
):
    devices = lax.axis_size("elem")
    tracers, levels, nodes, local = tracer_field.shape
    steps = 3 * (levels // SUB)
    f32 = jnp.float32
    vmem = pl.BlockSpec(memory_space=pltpu.VMEM)
    smem = pl.BlockSpec(memory_space=pltpu.SMEM)
    hbm = pl.BlockSpec(memory_space=pl.ANY)
    tall = levels + 2 * GUARD
    by_node, by_cell = pl.pallas_call(
        functools.partial(kernel, devices),
        out_shape=(
            jax.ShapeDtypeStruct((nodes, tracers, levels, local), f32),
            jax.ShapeDtypeStruct((tracers, 4, levels, local), f32),
        ),
        in_specs=[hbm, hbm, vmem, vmem, vmem, smem, smem, smem, smem],
        out_specs=(vmem, vmem),
        scratch_shapes=[
            pltpu.VMEM((nodes, tracers, levels, local), f32),
            pltpu.VMEM((nodes, tracers, levels, local), f32),
            pltpu.VMEM((nodes, 2, levels, local), f32),
            pltpu.VMEM((steps, nodes, tracers, SUB, local), f32),
            pltpu.VMEM((steps // 3, nodes, tracers, SUB, local), f32),
            pltpu.VMEM((2, steps, 4, tracers, SUB, local), f32),
            pltpu.VMEM((nodes, SUB, local), f32),
            pltpu.VMEM((4, SUB, local), f32),
            pltpu.VMEM((6, local, local), jnp.bfloat16),
            pltpu.VMEM((2, 8, local), f32),
            pltpu.VMEM((4, 4, tall, local), f32),
            pltpu.VMEM((6, 4, tall, local), f32),
            pltpu.SemaphoreType.DMA((2, nodes)),
            pltpu.SemaphoreType.DMA((2, steps)),
            pltpu.SemaphoreType.DMA((2, steps)),
            pltpu.SemaphoreType.DMA((2,)),
            pltpu.SemaphoreType.DMA((2,)),
            pltpu.SemaphoreType.DMA,
            pltpu.SemaphoreType.DMA,
        ],
        compiler_params=pltpu.CompilerParams(
            collective_id=0, has_side_effects=True, vmem_limit_bytes=40 * 2**20
        ),
    )(
        tracer_field, velocity, node_mass, neighbours, seam_flips,
        conv_in, bias_in, conv_out, bias_out,
    )
    return jnp.transpose(by_node, (1, 2, 0, 3)), jnp.transpose(by_cell, (0, 2, 1, 3))


def solution(mesh):
    return jax.shard_map(
        per_device,
        mesh=mesh,
        in_specs=(
            P(None, "lev", None, ("grp", "elem")),
            P(None, "lev", None, ("grp", "elem")),
            P(None, ("grp", "elem")),
            P(None, ("grp", "elem")),
            P(None, ("grp", "elem")),
            P(),
            P(),
            P(),
            P(),
        ),
        out_specs=(P(None, "lev", None, ("grp", "elem")), P(None, "lev", None, ("grp", "elem"))),
        check_vma=False,
    )
```

profile of v0, /device:TPU:0, one launch (start us, length us, event | category | flops | bytes accessed | tf_op | source)
XLA Modules:
  0.0 49.6 jit_solution(5186080460665037502)
XLA Ops:
  0.6 0.0 copy-start.7
  0.6 0.0 copy-start.5
  0.7 0.0 copy-start.6
  0.7 0.0 copy-start.4
  0.7 0.0 copy-start.3
  0.7 0.0 copy-start.2
  0.7 0.8 %copy.11.conv_in = f32[3,16,4]{2,1,0:T(8,128)S(1)} copy(f32[3,16,4]{1,2,0:T(4,128)} %param.14) | data formatting | bytes 1536 | tf_op args[5]
  1.5 0.0 copy-done.7
  1.5 0.0 copy-done.5
  1.5 0.0 copy-done.6
  1.5 0.0 copy-done.4
  1.5 0.0 copy-done.3
  1.5 0.0 copy-done.2
  1.6 0.0 copy-start
  1.6 1.1 %copy-done = f32[2,24,16,256]{3,2,1,0:T(8,128)S(1)} copy-done((f32[2,24,16,256]{3,2,1,0:T(8,128)S(1)}, f32[2,24,16,256]{3,2,1,0:T(8,128)}, u32[]{:S(2)}) %copy-start) | copy-done | bytes 786456
  2.7 0.0 copy-start.1
  2.7 1.1 %copy-done.1 = f32[2,24,16,256]{3,2,1,0:T(8,128)S(1)} copy-done((f32[2,24,16,256]{3,2,1,0:T(8,128)S(1)}, f32[2,24,16,256]{3,2,1,0:T(8,128)}, u32[]{:S(2)}) %copy-start.1) | copy-done | bytes 786456
  3.8 43.6 %shard_map.104 = (f32[16,2,24,256]{3,2,1,0:T(8,128)S(1)}, f32[2,4,24,256]{3,2,1,0:T(8,128)S(1)}) custom-call(f32[2,24,16,256]{3,2,1,0:T(8,128)S(1)} %copy-done, f32[2,24,16,256]{3,2,1,0:T(8,128)S(1)} %copy-done.1, f32[16,256]{1,0:T(8,128)S(1)} %copy-done.2, s32[4,256]{1,0:T(4,128)S(1)} %copy-done.3, s32[4,256]{1,0:T(4,128)S(1)} %copy-done.4, ...), custom_call_target="tpu_custom_call" | custom-call | tf_op jit(solution)/shard_map/pallas_call | solution.py:335
  47.5 1.3 %copy.12 = f32[2,24,16,256]{3,2,1,0:T(8,128)} copy(f32[2,24,16,256]{3,1,0,2:T(8,128)S(1)} %bitcast.2) | data formatting | bytes 1572864
  48.8 0.8 %copy.13 = f32[2,24,4,256]{3,2,1,0:T(4,128)} copy(f32[2,24,4,256]{3,1,2,0:T(8,128)S(1)} %bitcast.3) | data formatting | bytes 393216
Async XLA Ops:
  0.6 0.9 %copy-start.7 = (f32[2]{0:T(128)S(1)}, f32[2]{0:T(128)}, u32[]{:S(2)}) copy-start(f32[2]{0:T(128)} %bias_out.1) | copy-start | bytes 28
  0.6 0.9 %copy-start.5 = (f32[3,2,16]{2,1,0:T(2,128)S(1)}, f32[3,2,16]{2,1,0:T(2,128)}, u32[]{:S(2)}) copy-start(f32[3,2,16]{2,1,0:T(2,128)} %conv_out.1) | copy-start | bytes 1156
  0.7 0.9 %copy-start.6 = (f32[16]{0:T(128)S(1)}, f32[16]{0:T(128)}, u32[]{:S(2)}) copy-start(f32[16]{0:T(128)} %bias_in.1) | copy-start | bytes 196
  0.7 0.9 %copy-start.4 = (s32[4,256]{1,0:T(4,128)S(1)}, s32[4,256]{1,0:T(4,128)}, u32[]{:S(2)}) copy-start(s32[4,256]{1,0:T(4,128)} %flips.1) | copy-start | bytes 12292
  0.7 0.9 %copy-start.3 = (s32[4,256]{1,0:T(4,128)S(1)}, s32[4,256]{1,0:T(4,128)}, u32[]{:S(2)}) copy-start(s32[4,256]{1,0:T(4,128)} %nbr.1) | copy-start | bytes 12292
  0.7 0.9 %copy-start.2 = (f32[16,256]{1,0:T(8,128)S(1)}, f32[16,256]{1,0:T(8,128)}, u32[]{:S(2)}) copy-start(f32[16,256]{1,0:T(8,128)} %mass.1) | copy-start | bytes 49156
  1.6 1.1 %copy-start = (f32[2,24,16,256]{3,2,1,0:T(8,128)S(1)}, f32[2,24,16,256]{3,2,1,0:T(8,128)}, u32[]{:S(2)}) copy-start(f32[2,24,16,256]{3,2,1,0:T(8,128)} %tracer_in.1) | copy-start | bytes 2359300
  2.7 1.1 %copy-start.1 = (f32[2,24,16,256]{3,2,1,0:T(8,128)S(1)}, f32[2,24,16,256]{3,2,1,0:T(8,128)}, u32[]{:S(2)}) copy-start(f32[2,24,16,256]{3,2,1,0:T(8,128)} %velocity_in.1) | copy-start | bytes 2359300
where the time goes:
time: 49.8 us; the launch traced here: 49.6 us
  Pallas kernels  43.6 us (88%)
  local copies, waits for them, and re-layouts  5.19 us (10%)
  between operations  0.73 us (1%)
    pallas_call x1, Pallas kernels, per_device(): pl.pallas_call(functools.partial(kernel, devices), out_shape=(jax.ShapeDt...  43.6 us
    unnamed x19, local copies, waits for them, and re-layouts  5.19 us

commit v1 on v0

--- a/solution.py
+++ b/solution.py
@@ -47,8 +47,8 @@
 def kernel(
     devices, tracer_in, velocity_in, mass, nbr, flips, conv_in, bias_in, conv_out, bias_out,
     next_out, sub_out,
-    start, now, wind, weighted, base, landed, inv, cell_inv, tables, mass_land, features, partial,
-    in_sem, send_sem, recv_sem, mass_send_sem, mass_recv_sem, col_send_sem, col_recv_sem,
+    start, now, wind, weighted, base, landed, inv, cell_inv, tables, mass_land, features, totals,
+    first_net, second_net, in_sem, send_sem, recv_sem, mass_send_sem, mass_recv_sem, col_send_sem, col_recv_sem,
 ):
     local = mass.shape[1]
     levels = start.shape[2]
@@ -57,28 +57,28 @@
     me, lev = lax.axis_index("elem"), lax.axis_index("lev")
     after, before = lax.rem(me + 1, devices), lax.rem(me + devices - 1, devices)
 
-    loads = []
-    for node in range(16):
-        loads.append(
-            pltpu.make_async_copy(tracer_in.at[:, :, node, :], start.at[node], in_sem.at[0, node])
-        )
-        loads.append(
-            pltpu.make_async_copy(velocity_in.at[:, :, node, :], wind.at[node], in_sem.at[1, node])
-        )
-    for load in loads:
-        load.start()
+    def place(chunk):
+        return pl.multiple_of(jnp.where(lev == 0, chunks - 1 - chunk, chunk) * SUB, SUB)
+
+    def load_copies(chunk):
+        at = pl.ds(place(chunk), SUB)
+        return [
+            pltpu.make_async_copy(
+                source.at[:, at, node, :], target.at[node, :, at, :], in_sem.at[chunk, kind, node]
+            )
+            for kind, (source, target) in enumerate(((tracer_in, start), (velocity_in, wind)))
+            for node in range(16)
+        ]
+
+    def load(chunk, carry):
+        for copy in load_copies(chunk):
+            copy.start()
+        return carry
 
     barrier = pltpu.get_barrier_semaphore()
     for device in ({"elem": before}, {"elem": after}, {"lev": 1 - lev}):
         pl.semaphore_signal(barrier, inc=1, device_id=device, device_id_type=MESH)
-
-    rows = lax.broadcasted_iota(jnp.int32, (local, local), 0)
-    for slot, (edge, owner) in enumerate(
-        ((0, me), (1, me), (2, me), (3, me), (0, before), (2, after))
-    ):
-        wanted = nbr[pl.ds(edge, 1), :] - owner * local
-        tables[slot] = jnp.where(rows == wanted, 1.0, 0.0).astype(jnp.bfloat16)
-    pl.semaphore_wait(barrier, 3)
+    lax.fori_loop(0, chunks, load, 0)
 
     mass_copies = []
     for side, device in ((0, after), (1, before)):
@@ -92,7 +92,6 @@
                 device_id_type=MESH,
             )
         )
-        mass_copies[-1].start()
 
     def edge_copy(side, step):
         return pltpu.make_async_remote_copy(
@@ -103,9 +102,6 @@
             device_id={"elem": after if side == 0 else before},
             device_id_type=MESH,
         )
-
-    def place(chunk):
-        return pl.multiple_of(jnp.where(lev == 0, chunks - 1 - chunk, chunk) * SUB, SUB)
 
     def is_flipped(edge):
         return flips[pl.ds(edge, 1), :] == 1
@@ -121,8 +117,12 @@
                 weighted[step, node, tracer] = (
                     wind[node, 0, at, :] * along_x + wind[node, 1, at, :] * along_y
                 )
+
+    def send(step):
         edge_copy(0, step).start()
         edge_copy(1, step).start()
+
+    def gather_local(chunk, step):
         arrivals = [[] for _ in range(16)]
         for edge in range(4):
             theirs = EDGE_NODES[(edge + 2) % 4]
@@ -165,10 +165,9 @@
                 section = now[node, tracer, at, :] + TIME_STEP * inv[node] * total[tracer]
                 now[node, tracer, at, :] = keep * start[node, tracer, at, :] + blend * section
 
-    for load in loads:
-        load.wait()
-
-    def prepare(chunk, carry):
+    def prepare(chunk):
+        for copy in load_copies(chunk):
+            copy.wait()
         at = pl.ds(place(chunk), SUB)
         for node in range(16):
             node_mass = mass[pl.ds(node, 1), :]
@@ -177,9 +176,32 @@
             for tracer in range(2):
                 now[node, tracer, at, :] = start[node, tracer, at, :]
         slopes(start, chunk, chunk)
-        return carry
-
-    lax.fori_loop(0, chunks, prepare, 0)
+
+    prepare(0)
+    pl.semaphore_wait(barrier, 3)
+    for copy in mass_copies:
+        copy.start()
+    send(0)
+
+    def prepare_next(chunk, carry):
+        prepare(chunk)
+        send(chunk)
+        return carry
+
+    lax.fori_loop(1, chunks, prepare_next, 0)
+
+    rows = lax.broadcasted_iota(jnp.int32, (local, local), 0)
+    for slot, (edge, owner) in enumerate(
+        ((0, me), (1, me), (2, me), (3, me), (0, before), (2, after))
+    ):
+        wanted = nbr[pl.ds(edge, 1), :] - owner * local
+        tables[slot] = jnp.where(rows == wanted, 1.0, 0.0).astype(jnp.bfloat16)
+
+    def gather_first(chunk, carry):
+        gather_local(chunk, chunk)
+        return carry
+
+    lax.fori_loop(0, chunks, gather_first, 0)
 
     own_mass = mass[...]
     sums = [own_mass[node : node + 1] for node in range(16)]
@@ -213,26 +235,97 @@
         cell_mass = sum(own_mass[node : node + 1] for node in cells[cell])
         cell_inv[cell] = jnp.broadcast_to(1.0 / cell_mass, (SUB, local))
 
-    nothing = jnp.zeros((SUB, local), jnp.float32)
-    open_side = pl.multiple_of(jnp.where(lev == 0, GUARD - SUB, GUARD + levels), SUB)
-    for cell in range(4):
-        for channel in range(4):
-            features[channel, cell, pl.ds(0, SUB), :] = nothing
-            features[channel, cell, pl.ds(GUARD + levels + SUB, SUB), :] = nothing
-            features[channel, cell, pl.ds(open_side, SUB), :] = nothing
-        for kind in range(6):
-            partial[kind, cell, pl.ds(open_side, SUB), :] = nothing
+    def clear_columns():
+        nothing = jnp.zeros((SUB, local), jnp.float32)
+        open_side = pl.multiple_of(jnp.where(lev == 0, GUARD - SUB, GUARD + levels), SUB)
+        for cell in range(4):
+            for channel in range(4):
+                features[channel, cell, pl.ds(0, SUB), :] = nothing
+                features[channel, cell, pl.ds(GUARD + levels + SUB, SUB), :] = nothing
+                features[channel, cell, pl.ds(open_side, SUB), :] = nothing
+            for tracer in range(2):
+                totals[tracer, cell] = jnp.full(totals.shape[2:], bias_out[tracer], jnp.float32)
+
+    wide, deep = 4 * 3 * SUB, 16 * SUB
+
+    def split(table, columns):
+        second = lax.broadcasted_iota(jnp.int32, table.shape, 1) >= columns
+        high = table.astype(jnp.bfloat16)
+        low = jnp.where(second, 0.0, table - high.astype(jnp.float32)).astype(jnp.bfloat16)
+        return high, low
+
+    def build_nets():
+        col = lax.rem(lax.broadcasted_iota(jnp.int32, (SUB, 2 * wide), 1), wide)
+        row = lax.broadcasted_iota(jnp.int32, (SUB, 2 * wide), 0)
+        reach = lax.rem(col, 3 * SUB) - row - (SUB - 1)
+        masks = [
+            [jnp.where((reach == j) & (col // (3 * SUB) == i), 1.0, 0.0) for i in range(4)]
+            for j in range(3)
+        ]
+        for out in range(0, 16, 2):
+            pair = [
+                sum(conv_in[j, i, o] * masks[j][i] for j in range(3) for i in range(4))
+                for o in (out, out + 1)
+            ]
+            high, low = split(jnp.concatenate(pair, axis=0), wide)
+            first_net[pl.ds(SUB * out, 2 * SUB), :] = high
+            first_net[pl.ds(deep + SUB * out, 2 * SUB), :] = low
+        col = lax.rem(lax.broadcasted_iota(jnp.int32, (3 * SUB, 2 * deep), 1), deep)
+        row = lax.broadcasted_iota(jnp.int32, (3 * SUB, 2 * deep), 0)
+        reach = SUB + 1 + lax.rem(col, SUB) - row
+        bands = []
+        for tracer in range(2):
+            band = jnp.zeros((3 * SUB, 2 * deep), jnp.float32)
+            for o in range(16):
+                weight = jnp.zeros((3 * SUB, 2 * deep), jnp.float32)
+                for j in range(3):
+                    weight = jnp.where(reach == j, conv_out[j, tracer, o], weight)
+                band = jnp.where(col // SUB == o, weight, band)
+            bands.append(band)
+        high, low = split(jnp.concatenate(bands, axis=0), deep)
+        second_net[pl.ds(0, 6 * SUB), :] = high
+        second_net[pl.ds(6 * SUB, 6 * SUB), :] = low
+
+    def applied(net, values):
+        high = values.astype(jnp.bfloat16)
+        low = (values - high.astype(jnp.float32)).astype(jnp.bfloat16)
+        both = jnp.dot(
+            net[...], jnp.concatenate([high, low], axis=0), preferred_element_type=jnp.float32
+        )
+        half = both.shape[0] // 2
+        return both[:half] + both[half:]
+
+    def column_net(at):
+        window = pl.ds(pl.multiple_of(at - SUB, SUB), 3 * SUB)
+
+        for cell in range(4):
+            values = features[:, cell, window, :].reshape(wide, local)
+            hidden = applied(first_net, values)
+            hidden = jnp.concatenate(
+                [hidden[SUB * o : SUB * (o + 1)] + bias_in[o] for o in range(16)], axis=0
+            )
+            hidden = hidden / (1.0 + jnp.exp(-hidden))
+            terms = applied(second_net, hidden)
+            totals[:, cell, window, :] += terms.reshape(2, 3 * SUB, local)
 
     def section_step(index, carry):
         chunk = lax.rem(index, chunks)
-        first, second = index < chunks, index < 2 * chunks
-        keep = jnp.where(first, 0.0, jnp.where(second, 0.75, 1.0 / 3.0)).astype(jnp.float32)
-        blend = jnp.where(first, 1.0, jnp.where(second, 0.25, 2.0 / 3.0)).astype(jnp.float32)
+        first = index < chunks
+        keep = jnp.where(first, 0.0, 0.75).astype(jnp.float32)
+        blend = jnp.where(first, 1.0, 0.25).astype(jnp.float32)
         finish(chunk, index, keep, blend)
 
-        @pl.when(second)
+        slopes(now, chunk, index + chunks)
+        send(index + chunks)
+        gather_local(chunk, index + chunks)
+
+        @pl.when(index == 1)
         def _():
-            slopes(now, chunk, index + chunks)
+            clear_columns()
+
+        @pl.when(index == chunks)
+        def _():
+            build_nets()
 
         return carry
 
@@ -270,46 +363,22 @@
         def _():
             column_copy.start()
 
+        @pl.when(chunk == 1)
+        def _():
+            column_copy.wait()
+            column_net(jnp.where(lev == 0, GUARD + levels, GUARD - SUB))
+
+        @pl.when(chunk >= 1)
+        def _():
+            column_net(GUARD + place(chunk - 1))
+
         return carry
 
     lax.fori_loop(2 * chunks, 3 * chunks, last_step, 0)
-    column_copy.wait()
-
-    def column_net(index, carry):
-        chunk, cell = index // 4, lax.rem(index, 4)
-        inner = GUARD + chunk * SUB
-        border = jnp.where(lev == 0, GUARD + levels, GUARD - SUB)
-        at = pl.multiple_of(jnp.where(chunk < chunks, inner, border), SUB)
-        inputs = []
-        for channel in range(4):
-            whole = features[channel, cell, pl.ds(pl.multiple_of(at - SUB, SUB), 3 * SUB), :]
-            inputs.append([whole[SUB - 1 + j : 2 * SUB - 1 + j] for j in range(3)])
-        totals = [None] * 6
-        for out in range(16):
-            value = bias_in[out]
-            for j in range(3):
-                for channel in range(4):
-                    value = value + conv_in[j, out, channel] * inputs[channel][j]
-            value = value / (1.0 + jnp.exp(-value))
-            for j in range(3):
-                for tracer in range(2):
-                    term = conv_out[j, tracer, out] * value
-                    kind = 2 * j + tracer
-                    totals[kind] = term if totals[kind] is None else totals[kind] + term
-        for kind in range(6):
-            partial[kind, cell, pl.ds(at, SUB), :] = totals[kind]
-        return carry
-
-    lax.fori_loop(0, 4 * (chunks + 1), column_net, 0)
-
+    column_net(GUARD + place(chunks - 1))
     for cell in range(4):
         for tracer in range(2):
-            sub_out[tracer, cell] = (
-                bias_out[tracer]
-                + partial[tracer, cell, pl.ds(GUARD - 1, levels), :]
-                + partial[2 + tracer, cell, pl.ds(GUARD, levels), :]
-                + partial[4 + tracer, cell, pl.ds(GUARD + 1, levels), :]
-            )
+            sub_out[tracer, cell] = totals[tracer, cell, pl.ds(GUARD, levels), :]
 
     def drain(index, carry):
         edge_copy(0, index).wait_send()
@@ -317,6 +386,7 @@
         return carry
 
     lax.fori_loop(0, 3 * chunks, drain, 0)
+
     for side in range(2):
         mass_copies[side].wait_send()
 
@@ -352,8 +422,10 @@
             pltpu.VMEM((6, local, local), jnp.bfloat16),
             pltpu.VMEM((2, 8, local), f32),
             pltpu.VMEM((4, 4, tall, local), f32),
-            pltpu.VMEM((6, 4, tall, local), f32),
-            pltpu.SemaphoreType.DMA((2, nodes)),
+            pltpu.VMEM((2, 4, tall, local), f32),
+            pltpu.VMEM((2 * 16 * SUB, 2 * 4 * 3 * SUB), jnp.bfloat16),
+            pltpu.VMEM((2 * 2 * 3 * SUB, 2 * 16 * SUB), jnp.bfloat16),
+            pltpu.SemaphoreType.DMA((levels // SUB, 2, nodes)),
             pltpu.SemaphoreType.DMA((2, steps)),
             pltpu.SemaphoreType.DMA((2, steps)),
             pltpu.SemaphoreType.DMA((2,)),
@@ -362,11 +434,11 @@
             pltpu.SemaphoreType.DMA,
         ],
         compiler_params=pltpu.CompilerParams(
-            collective_id=0, has_side_effects=True, vmem_limit_bytes=40 * 2**20
+            collective_id=0, has_side_effects=True, vmem_limit_bytes=60 * 2**20
         ),
     )(
         tracer_field, velocity, node_mass, neighbours, seam_flips,
-        conv_in, bias_in, conv_out, bias_out,
+        jnp.transpose(conv_in, (0, 2, 1)), bias_in, conv_out, bias_out,
     )
     return jnp.transpose(by_node, (1, 2, 0, 3)), jnp.transpose(by_cell, (0, 2, 1, 3))
 

time: 49.8 us -> 42.5 us (0.85)
  Pallas kernels: 43.6 us -> 38.3 us
  local copies, waits for them, and re-layouts: 5.19 us -> 3.27 us
    pallas_call x1, Pallas kernels: 43.6 us -> 38.3 us  [per_device(): pl.pallas_call(functools.partial(kernel, devices), out_shape=(jax.ShapeDt...]
    unnamed x19 -> x4, local copies, waits for them, and re-layouts: 5.19 us -> 3.27 us
where the time goes in v1:
time: 42.5 us; the launch traced here: 42.2 us
  Pallas kernels  38.3 us (90%)
  local copies, waits for them, and re-layouts  3.27 us (8%)
  between operations  0.65 us (2%)
    pallas_call x1, Pallas kernels, per_device(): pl.pallas_call(functools.partial(kernel, devices), out_shape=(jax.ShapeDt...  38.3 us
    unnamed x4, local copies, waits for them, and re-layouts  3.27 us

profile of v1, /device:TPU:0, one launch (start us, length us, event | category | flops | bytes accessed | tf_op | source)
XLA Modules:
  0.0 42.2 jit_solution(440574695160251428)
XLA Ops:
  0.6 38.3 %shard_map.104 = (f32[16,2,24,256]{3,2,1,0:T(8,128)}, f32[2,4,24,256]{3,2,1,0:T(8,128)}) custom-call(f32[2,24,16,256]{3,2,1,0:T(8,128)} %tracer_in.1, f32[2,24,16,256]{3,2,1,0:T(8,128)} %velocity_in.1, f32[16,256]{1,0:T(8,128)} %mass.1, s32[4,256]{1,0:T(4,128)} %nbr.1, s32[4,256]{1,0:T(4,128)} %flips.1, f32[3,4,16]{2,1,0:T(4,128)} %bitcast.5, f32[16]{0:T(128)} %bias_in.1, ...), custom_call_target="tpu_custom_call" | custom-call | tf_op jit(solution)/shard_map/pallas_call | solution.py:405
  38.9 0.0 copy-start
  38.9 2.5 %copy.11 = f32[2,24,16,256]{3,2,1,0:T(8,128)} copy(f32[2,24,16,256]{3,1,0,2:T(8,128)} %bitcast.3) | data formatting | bytes 1572864
  41.4 0.0 copy-done
  41.4 0.8 %copy.12 = f32[2,24,4,256]{3,2,1,0:T(4,128)} copy(f32[2,24,4,256]{3,1,2,0:T(8,128)S(1)} %bitcast.4) | data formatting | bytes 393216
Async XLA Ops:
  38.9 2.5 %copy-start = (f32[2,4,24,256]{3,2,1,0:T(8,128)S(1)}, f32[2,4,24,256]{3,2,1,0:T(8,128)}, u32[]{:S(2)}) copy-start(f32[2,4,24,256]{3,2,1,0:T(8,128)} %get-tuple-element.5) | copy-start | bytes 589828
